TPU v7x, 32 devices: a whole 2x2x4 slice. The times are simulated.
32 devices in a mesh: expert: 4 (over y, x), fsdp: 8 (over z, core).
Axes of the slice: x: 2, y: 2, z: 4, core: 2. Of those that a mesh axis runs over, the one named last changes fastest.
Arguments:
- tokens: bfloat16 [4608, 2048], P(('expert', 'fsdp')), may hold values from -6 to 6
- expert_ids: int32 [4608, 6], P(('expert', 'fsdp')), may hold values from 0 to 15, as said below
- combine: float32 [4608, 6], P(('expert', 'fsdp')), may hold values from 0.05 to 1
- gate_weight: bfloat16 [16, 1408, 2048], P('expert', 'fsdp'), may hold values from -0.125 to 0.125
- up_weight: bfloat16 [16, 1408, 2048], P('expert', 'fsdp'), may hold values from -0.125 to 0.125
- down_weight: bfloat16 [16, 1408, 2048], P('expert', 'fsdp'), may hold values from -0.15625 to 0.15625
Outputs:
- mixed: bfloat16 [4608, 2048], P(('expert', 'fsdp'))
Inputs may be any that keep to these rules, and one draw needn't show every extreme that they name: `expert_ids`: each row names 6 different experts. Within the 144 rows of each device no expert is named more than 72 times, and one and the same expert is named exactly 72 times by the rows of every device.
All inputs are finite; a program needn't handle non-finite values.
Results may differ from a plain program's by a relative error of at most 0.0058.
Values may be sent and summed in bfloat16 or wider, within the bound.
No kernel may reach another device: no remote copies, remote signals or barrier semaphores. Data moves between devices by JAX's collectives and lax.ppermute only.
A program may use at most 128 MiB of HBM per device.

v0:
```python
import functools

import jax
import jax.numpy as jnp
from jax import lax
from jax.experimental import pallas as pl
from jax.experimental.pallas import tpu as pltpu
from jax.sharding import Mesh, PartitionSpec as P

AXES = ("e_hi", "e_lo", "line", "core")
LANES = 128
TILE = 256


def tiles(extent, size=TILE):
    return [(at, min(size, extent - at)) for at in range(0, extent, size)]


def ffn_kernel(ny, nx, experts, per_group, *refs):
    first, refs = refs[0], refs[1:]
    near, refs = refs[: nx + ny - 2], refs[nx + ny - 2 :]
    left, right, refs = refs[: ny - 1], refs[ny - 1 : ny + nx - 2], refs[ny + nx - 2 :]
    weights, refs = refs[:6], refs[6:]
    send_a, keep_a, send_b, keep_b = refs[:4]
    rows, hidden, row_sem = refs[4:]
    count, depth = rows.shape[0], weights[0].shape[1]
    half = depth // 2
    units = weights[0].shape[0]
    tok = count // (ny * nx)
    group = lax.axis_index("e_hi") * nx + lax.axis_index("e_lo")

    row_copies = []

    def bring(source, from_row, block, low):
        cols = pl.ds(0, half) if low else pl.ds(half, rows.shape[1] - half)
        from_cols = cols if source.shape[1] == rows.shape[1] else pl.ds(0, source.shape[1])
        row_copies.append(
            pltpu.make_async_copy(
                source.at[pl.ds(from_row, tok), from_cols],
                rows.at[pl.ds(block * tok, tok), cols],
                row_sem.at[len(row_copies)],
            )
        )

    for jy in range(ny):
        for jx in range(nx):
            block = jy * nx + jx
            if jy:
                bring(left[jy - 1], jx * tok, block, True)
            else:
                bring(near[jx - 1] if jx else first, 0, block, True)
            if jx:
                bring(right[jx - 1], jy * tok, block, False)
            else:
                bring(near[nx - 1 + jy - 1] if jy else first, 0, block, False)
    for copy in row_copies:
        copy.start()
    for copy in row_copies:
        copy.wait()

    extra = rows[:, depth:].astype(jnp.float32)
    lane = lax.broadcasted_iota(jnp.int32, extra.shape, 1)
    named = []
    for e in range(per_group):
        mine = group * per_group + e
        pick = (lane == mine) | (lane == mine + experts)
        named.append(0.5 * jnp.sum(jnp.where(pick, extra, 0.0), axis=1, keepdims=True))

    per_expert = units // per_group
    nt = (((1,), (1,)), ((), ()))
    for h in range(2):
        gate, up = weights[3 * h], weights[3 * h + 1]
        for start, size in tiles(units):
            gate_pre = lax.dot_general(
                rows[:, :depth],
                gate[start : start + size],
                nt,
                preferred_element_type=jnp.float32,
            )
            up_pre = lax.dot_general(
                rows[:, :depth],
                up[start : start + size],
                nt,
                preferred_element_type=jnp.float32,
            )
            low, high = start // per_expert, (start + size - 1) // per_expert
            column = lax.broadcasted_iota(jnp.int32, (1, size), 1) + start
            scale = named[high]
            for e in range(high - 1, low - 1, -1):
                scale = jnp.where(column < (e + 1) * per_expert, named[e], scale)
            value = gate_pre * (1.0 + jnp.tanh(0.5 * gate_pre)) * (up_pre * scale)
            hidden[h, :, start : start + size] = value.astype(jnp.bfloat16)

    def down_product(start):
        cols = pl.ds(pl.multiple_of(start, TILE), TILE)
        return sum(
            jnp.dot(hidden[h], weights[3 * h + 2][:, cols], preferred_element_type=jnp.float32)
            for h in range(2)
        )

    @pl.loop(0, half // TILE)
    def _(step):
        part = down_product(step * TILE)
        to = pl.ds(pl.multiple_of(step * TILE, TILE), TILE)
        for jy in range(ny):
            block = part[jy * nx * tok : (jy + 1) * nx * tok]
            if jy:
                send_a[jy - 1, :, to] = block.astype(jnp.bfloat16)
            else:
                keep_a[:, to] = block

    @pl.loop(0, half // TILE)
    def _(step):
        part = down_product(half + step * TILE)
        to = pl.ds(pl.multiple_of(step * TILE, TILE), TILE)
        for jy in range(ny):
            for jx in range(nx):
                at = (jy * nx + jx) * tok
                block = part[at : at + tok]
                there = slice(jy * tok, (jy + 1) * tok)
                if jx:
                    send_b[jx - 1, there, to] = block.astype(jnp.bfloat16)
                else:
                    keep_b[there, to] = block


def ffn(first, near, left, right, weights, experts, per_group):
    ny, nx = len(left) + 1, len(right) + 1
    tok, width = first.shape
    units, depth = weights[0].shape
    half, count = depth // 2, ny * nx * tok
    any_spec, vmem = pl.BlockSpec(memory_space=pl.ANY), pl.BlockSpec(memory_space=pltpu.VMEM)
    sources = [first, *near, *left, *right]
    macs = count * depth * units * 6
    return pl.pallas_call(
        functools.partial(ffn_kernel, ny, nx, experts, per_group),
        in_specs=[any_spec] * len(sources) + [vmem] * 6,
        out_specs=[vmem] * 4,
        out_shape=[
            jax.ShapeDtypeStruct((ny - 1, nx * tok, half), jnp.bfloat16),
            jax.ShapeDtypeStruct((nx * tok, half), jnp.float32),
            jax.ShapeDtypeStruct((nx - 1, ny * tok, half), jnp.bfloat16),
            jax.ShapeDtypeStruct((ny * tok, half), jnp.float32),
        ],
        scratch_shapes=[
            pltpu.VMEM((count, width), jnp.bfloat16),
            pltpu.VMEM((2, count, units), jnp.bfloat16),
            pltpu.SemaphoreType.DMA((2 * ny * nx,)),
        ],
        compiler_params=pltpu.CompilerParams(vmem_limit_bytes=14 * 1024 * 1024),
        cost_estimate=pl.CostEstimate(
            flops=2 * macs,
            bytes_accessed=8 * count * depth,
            transcendentals=2 * count * units,
        ),
    )(*sources, *weights)


def shift(value, axis, by):
    n = lax.axis_size(axis)
    return lax.ppermute(value, axis, [(i, (i + by) % n) for i in range(n)])


def ring_step(value):
    n = lax.axis_size("line")
    order = list(range(1, n, 2)) + list(range(0, n, 2))[::-1]
    return lax.ppermute(value, "line", [(order[i], order[(i + 1) % n]) for i in range(n)])


def after(value, *earlier):
    return lax.optimization_barrier((value, earlier))[0]


def per_device(tokens, expert_ids, combine, gate_weight, up_weight, down_weight):
    ny, nx, stages = lax.axis_size("e_hi"), lax.axis_size("e_lo"), lax.axis_size("line")
    per_group, units, depth = gate_weight.shape
    experts = ny * nx * per_group
    tok = tokens.shape[0]
    half = depth // 2

    chosen = expert_ids[:, :, None] == jnp.arange(experts, dtype=jnp.int32)[None, None, :]
    named = jnp.sum(jnp.where(chosen, combine[:, :, None], 0.0), axis=1)
    high = named.astype(jnp.bfloat16)
    rest = (named - high.astype(jnp.float32)).astype(jnp.bfloat16)
    pad = jnp.zeros((tok, LANES * -(-2 * experts // LANES) - 2 * experts), jnp.bfloat16)
    first = jnp.concatenate([tokens, high, rest, pad], axis=1)

    def near_of(pieces):
        if nx == ny:
            lefts, rights = pieces[: nx - 1], pieces[nx - 1 :]
            return [jnp.concatenate([a, b], axis=1) for a, b in zip(lefts, rights)]
        return pieces

    def halves_of(near):
        if nx == ny:
            return [n[:, :half] for n in near], [n[:, half:] for n in near]
        return near[: nx - 1], near[nx - 1 :]

    near = [shift(tokens[:, :half], "e_lo", j) for j in range(1, nx)]
    near += [shift(first[:, half:], "e_hi", j) for j in range(1, ny)]
    near = near_of(near)

    own = [w.reshape(per_group * units, depth) for w in (gate_weight, up_weight, down_weight)]
    other = [shift(own[0], "core", 1)]

    def add(*terms):
        return sum(t.astype(jnp.float32) for t in terms)

    def exchange(first, near):
        lefts, rights = halves_of(near)
        left = jnp.concatenate([first[:, :half], *lefts])
        right = jnp.concatenate([first[:, half:], *rights])
        return (
            [shift(left, "e_hi", j) for j in range(1, ny)],
            [shift(right, "e_lo", j) for j in range(1, nx)],
        )

    def run(first, near, sides, *earlier):
        first, sides = after((first, sides), *earlier)
        if nx == ny:
            lefts, rights = halves_of(near)
            near = lefts + rights
        return ffn(first, near, *sides, weights, experts, per_group)

    def start_sums(parts, *earlier):
        send_a, keep_a, send_b, keep_b = parts
        send_a, send_b = after((send_a, send_b), *earlier)
        got_a = [shift(send_a[j - 1], "e_hi", -j) for j in range(1, ny)]
        got_b = [shift(send_b[j - 1], "e_lo", -j) for j in range(1, nx)]
        return [keep_a] + got_a, [keep_b] + got_b

    def finish_sums(terms_a, terms_b):
        sum_a = add(*terms_a).reshape(nx, tok, half)
        sum_b = add(*terms_b).reshape(ny, tok, half)
        last_a = [shift(sum_a[j].astype(jnp.bfloat16), "e_lo", -j) for j in range(1, nx)]
        last_b = [shift(sum_b[j].astype(jnp.bfloat16), "e_hi", -j) for j in range(1, ny)]
        return [sum_a[0]] + last_a, [sum_b[0]] + last_b

    firsts, nears, sides = [first], [near], [exchange(first, near)]
    firsts.append(ring_step(first))
    nears.append([ring_step(n) for n in near])
    other.append(shift(after(own[1], other[0], near, firsts[1]), "core", 1))
    other.append(shift(after(own[2], other[0], near, firsts[1]), "core", 1))
    weights = own + other

    parts, begun = {}, {}
    for k in range(1, stages):
        sides.append(exchange(firsts[k], nears[k]))
        if k + 1 < stages:
            if nx == ny:
                pair = jnp.concatenate([firsts[k], *nears[k]])
                pair = ring_step(pair)
                firsts.append(pair[:tok])
                nears.append([pair[i * tok : (i + 1) * tok] for i in range(1, nx)])
            else:
                firsts.append(ring_step(firsts[k]))
                nears.append([ring_step(n) for n in nears[k]])
        earlier = firsts[k], nears[k], begun.get(k - 2)
        parts[k - 1] = run(firsts[k - 1], nears[k - 1], sides[k - 1], *earlier)
        begun[k - 1] = start_sums(parts[k - 1], sides[k])
    last = stages - 1
    parts[last] = run(
        firsts[last], nears[last], sides[last], parts[last - 1], begun[last - 2]
    )
    begun[last] = start_sums(parts[last], begun[last - 1])

    carry_a, carry_b = [], []
    for k in list(range(1, stages)) + [0]:
        terms_a, terms_b = begun[k]
        if k == 1:
            sums = jnp.concatenate([add(*terms_a), add(*terms_b)], axis=1 if nx == ny else 0)
            sums = ring_step(sums.astype(jnp.bfloat16))
            if nx == ny:
                mid_a, mid_b = [sums[:, :half]], [sums[:, half:]]
            else:
                mid_a, mid_b = [sums[: nx * tok]], [sums[nx * tok :]]
            continue
        if k == 0:
            mid_a, mid_b = [], []
        a, b = finish_sums(terms_a + mid_a, terms_b + mid_b)
        mid_a, mid_b = [], []
        total = jnp.concatenate([add(*a, *carry_a), add(*b, *carry_b)], axis=1)
        total = total.astype(jnp.bfloat16)
        if k:
            total = ring_step(total)
            carry_a, carry_b = [total[:, :half]], [total[:, half:]]
    return total


def solution(mesh):
    groups, shards = mesh.shape["expert"], mesh.shape["fsdp"]
    split = Mesh(mesh.devices.reshape(groups // 2, 2, shards // 2, 2), AXES)
    whole, expert, shard = P(AXES, None), ("e_hi", "e_lo"), ("line", "core")
    return jax.shard_map(
        per_device,
        mesh=split,
        in_specs=(whole, whole, whole) + (P(expert, shard, None),) * 3,
        out_specs=whole,
        check_vma=False,
    )
```

profile of v0, /device:TPU:0, one launch (start us, length us, event | category | flops | bytes accessed | tf_op | source)
XLA Modules:
  0.0 187.7 jit_solution(5980833750915986390)
XLA Ops:
  0.5 1.0 slice.135
  1.4 2.6 %collective-permute-start = (bf16[144,1024]{1,0:T(8,128)(2,1)S(1)}, bf16[144,1024]{1,0:T(8,128)(2,1)S(1)}, u32[]{:S(2)}, u32[]{:S(2)}) collective-permute-start(bf16[144,1024]{1,0:T(8,128)(2,1)S(1)} %slice.135), channel_id=1, source_target_pairs={{0,8},{8,0},{1,9},{9,1},{2,10},{10,2},{3,11},{11,3},{4,12},{12,4},... | collective-permute-start | bytes 884744 | tf_op jit(solution)/shard_map/ppermute | solution.py:161
  4.1 0.7 select_reduce_fusion
  5.4 1.6 collective-permute-start.4
  7.0 1.6 collective-permute-start.2
  8.6 3.1 %collective-permute-done.refs_1_ = bf16[144,1024]{1,0:T(8,128)(2,1)S(1)} collective-permute-done((bf16[144,1024]{1,0:T(8,128)(2,1)S(1)}, bf16[144,1024]{1,0:T(8,128)(2,1)S(1)}, u32[]{:S(2)}, u32[]{:S(2)}) %collective-permute-start) | collective-permute-done | bytes 294944 | tf_op jit(solution)/shard_map/ppermute | solution.py:161
  11.7 5.0 %collective-permute-done.2.refs_2_ = bf16[144,1152]{1,0:T(8,128)(2,1)S(1)} collective-permute-done((bf16[144,1152]{1,0:T(8,128)(2,1)S(1)}, bf16[144,1152]{1,0:T(8,128)(2,1)S(1)}, u32[]{:S(2)}, u32[]{:S(2)}) %collective-permute-start.2) | collective-permute-done | bytes 331808 | tf_op jit(solution)/shard_map/ppermute | solution.py:161
  16.7 5.8 %collective-permute-done.4.refs_0_ = bf16[144,2176]{1,0:T(8,128)(2,1)S(1)} collective-permute-done((bf16[144,2176]{1,0:T(8,128)(2,1)S(1)}, bf16[144,2176]{1,0:T(8,128)(2,1)S(1)}, u32[]{:S(2)}, u32[]{:S(2)}) %collective-permute-start.4) | collective-permute-done | bytes 626720 | tf_op jit(solution)/shard_map/ppermute | solution.py:167
  23.0 0.8 collective-permute-start.5
  23.8 1.6 collective-permute-start.1
  25.5 0.6 collective-permute-start.3
  26.1 13.9 %collective-permute-done.5 = bf16[144,2176]{1,0:T(8,128)(2,1)S(1)} collective-permute-done((bf16[144,2176]{1,0:T(8,128)(2,1)S(1)}, bf16[144,2176]{1,0:T(8,128)(2,1)S(1)}, u32[]{:S(2)}, u32[]{:S(2)}) %collective-permute-start.5) | collective-permute-done | bytes 626720 | tf_op jit(solution)/shard_map/ppermute | solution.py:167
  40.1 1.6 collective-permute-start.9
  41.9 0.6 collective-permute-start.10
  42.5 3.6 %collective-permute-start.13 = (bf16[288,2176]{1,0:T(8,128)(2,1)S(1)}, bf16[288,2176]{1,0:T(8,128)(2,1)S(1)}, u32[]{:S(2)}, u32[]{:S(2)}) collective-permute-start(bf16[288,2176]{1,0:T(8,128)(2,1)S(1)} %pad_maximum_fusion), channel_id=1, source_target_pairs={{2,6},{6,4},{4,0},{0,2},{3,7},{7,5},{5,1},{1,3},{10,14},{14,12},{1... | collective-permute-start | bytes 3760136 | tf_op jit(solution)/shard_map/ppermute | solution.py:167
  46.2 14.8 %shard_map.64 = (bf16[1,288,1024]{2,1,0:T(8,128)(2,1)S(1)}, f32[288,1024]{1,0:T(8,128)S(1)}, bf16[1,288,1024]{2,1,0:T(8,128)(2,1)S(1)}, f32[288,1024]{1,0:T(8,128)S(1)}) custom-call(bf16[144,2176]{1,0:T(8,128)(2,1)S(1)} %concatenate.50.refs_0_, bf16[144,1024]{1,0:T(8,128)(2,1)S(1)} %collective-permute-done.refs_1_, ...), custom_call_target="tpu_custom_call" | custom-call | flops 9965666304 | bytes 9437184 | tf_op jit(solution)/shard_map/pallas_call | solution.py:135
  61.1 0.6 collective-permute-start.19
  61.7 9.9 %collective-permute-done.13 = bf16[288,2176]{1,0:T(8,128)(2,1)S(1)} collective-permute-done((bf16[288,2176]{1,0:T(8,128)(2,1)S(1)}, bf16[288,2176]{1,0:T(8,128)(2,1)S(1)}, u32[]{:S(2)}, u32[]{:S(2)}) %collective-permute-start.13) | collective-permute-done | bytes 1253408 | tf_op jit(solution)/shard_map/ppermute | solution.py:167
  71.6 1.2 collective-permute-start.17
  72.9 1.6 collective-permute-start.18
  74.4 0.8 collective-permute-start.14
  75.4 14.8 %shard_map.65 = (bf16[1,288,1024]{2,1,0:T(8,128)(2,1)S(1)}, f32[288,1024]{1,0:T(8,128)S(1)}, bf16[1,288,1024]{2,1,0:T(8,128)(2,1)S(1)}, f32[288,1024]{1,0:T(8,128)S(1)}) custom-call(bf16[144,2176]{1,0:T(8,128)(2,1)S(1)} %copy-done.1, bf16[144,1024]{1,0:T(8,128)(2,1)S(1)} %slice.167.refs_1_, bf16[144,1152]{1,0:T(8,128)(2,1)S(1)} %slice.169.refs_2_, ...), custom_call_target="tpu_custom_call" | custom-call | flops 9965666304 | bytes 9437184 | tf_op jit(solution)/shard_map/pallas_call | solution.py:135
  90.2 1.7 collective-permute-start.20
  91.9 0.7 collective-permute-start.21
  92.6 9.6 %collective-permute-done.14 = bf16[288,2176]{1,0:T(8,128)(2,1)S(1)} collective-permute-done((bf16[288,2176]{1,0:T(8,128)(2,1)S(1)}, bf16[288,2176]{1,0:T(8,128)(2,1)S(1)}, u32[]{:S(2)}, u32[]{:S(2)}) %collective-permute-start.14) | collective-permute-done | bytes 1253408 | tf_op jit(solution)/shard_map/ppermute | solution.py:167
  102.3 0.7 collective-permute-start.15
  103.0 0.6 collective-permute-start.16
  104.5 6.2 %collective-permute-start.26 = (bf16[288,2048]{1,0:T(8,128)(2,1)S(1)}, bf16[288,2048]{1,0:T(8,128)(2,1)S(1)}, u32[]{:S(2)}, u32[]{:S(2)}) collective-permute-start(bf16[288,2048]{1,0:T(8,128)(2,1)S(1)} %pad_maximum_fusion.1), channel_id=1, source_target_pairs={{2,6},{6,4},{4,0},{0,2},{3,7},{7,5},{5,1},{1,3},{10,14},{14,12},{1... | collective-permute-start | bytes 3538952 | tf_op jit(solution)/shard_map/ppermute | solution.py:167
  110.8 14.8 %shard_map.66 = (bf16[1,288,1024]{2,1,0:T(8,128)(2,1)S(1)}, f32[288,1024]{1,0:T(8,128)S(1)}, bf16[1,288,1024]{2,1,0:T(8,128)(2,1)S(1)}, f32[288,1024]{1,0:T(8,128)S(1)}) custom-call(bf16[144,2176]{1,0:T(8,128)(2,1)S(1)} %slice.173.refs_0_, bf16[144,1024]{1,0:T(8,128)(2,1)S(1)} %slice.174.refs_1_, bf16[144,1152]{1,0:T(8,128)(2,1)S(1)} %slice.175.refs_2_, ...), custom_call_target="tpu_custom_call" | custom-call | flops 9965666304 | bytes 9437184 | tf_op jit(solution)/shard_map/pallas_call | solution.py:135
  125.6 1.2 collective-permute-start.22
  127.3 15.0 %shard_map.67 = (bf16[1,288,1024]{2,1,0:T(8,128)(2,1)S(1)}, f32[288,1024]{1,0:T(8,128)S(1)}, bf16[1,288,1024]{2,1,0:T(8,128)(2,1)S(1)}, f32[288,1024]{1,0:T(8,128)S(1)}) custom-call(bf16[144,2176]{1,0:T(8,128)(2,1)S(1)} %slice.172.refs_0_, bf16[144,1024]{1,0:T(8,128)(2,1)S(1)} %slice.176.refs_1_, bf16[144,1152]{1,0:T(8,128)(2,1)S(1)} %slice.177.refs_2_, ...), custom_call_target="tpu_custom_call" | custom-call | flops 9965666304 | bytes 9437184 | tf_op jit(solution)/shard_map/pallas_call | solution.py:135
  142.4 1.0 collective-permute-start.24
  143.4 1.5 collective-permute-start.30
  145.5 1.2 collective-permute-start.28
  147.3 5.1 %collective-permute-done.24 = bf16[288,1024]{1,0:T(8,128)(2,1)S(1)} collective-permute-done((bf16[288,1024]{1,0:T(8,128)(2,1)S(1)}, bf16[288,1024]{1,0:T(8,128)(2,1)S(1)}, u32[]{:S(2)}, u32[]{:S(2)}) %collective-permute-start.24) | collective-permute-done | bytes 589856 | tf_op jit(solution)/shard_map/ppermute | solution.py:161
  152.6 1.8 collective-permute-start.25
  154.4 2.1 %collective-permute-done.28 = bf16[144,1024]{1,0:T(8,128)(2,1)S(1)} collective-permute-done((bf16[144,1024]{1,0:T(8,128)(2,1)S(1)}, bf16[144,1024]{1,0:T(8,128)(2,1)S(1)}, u32[]{:S(2)}, u32[]{:S(2)}) %collective-permute-start.28) | collective-permute-done | bytes 294944 | tf_op jit(solution)/shard_map/ppermute | solution.py:161
  156.5 5.3 %collective-permute-done.27 = bf16[144,1024]{1,0:T(8,128)(2,1)S(1)} collective-permute-done((bf16[144,1024]{1,0:T(8,128)(2,1)S(1)}, bf16[144,1024]{1,0:T(8,128)(2,1)S(1)}, u32[]{:S(2)}, u32[]{:S(2)}) %collective-permute-start.27) | collective-permute-done | bytes 294944 | tf_op jit(solution)/shard_map/ppermute | solution.py:161
  161.9 3.0 %collective-permute-start.29 = (bf16[144,2048]{1,0:T(8,128)(2,1)S(1)}, bf16[144,2048]{1,0:T(8,128)(2,1)S(1)}, u32[]{:S(2)}, u32[]{:S(2)}) collective-permute-start(bf16[144,2048]{1,0:T(8,128)(2,1)S(1)} %pad_maximum_fusion.6), channel_id=1, source_target_pairs={{2,6},{6,4},{4,0},{0,2},{3,7},{7,5},{5,1},{1,3},{10,14},{14,12},{1... | collective-permute-start | bytes 1769480 | tf_op jit(solution)/shard_map/ppermute | solution.py:167
  165.1 1.7 collective-permute-start.31
  167.1 0.6 collective-permute-start.12
  167.7 4.2 %collective-permute-done.31 = bf16[144,1024]{1,0:T(8,128)(2,1)S(1)} collective-permute-done((bf16[144,1024]{1,0:T(8,128)(2,1)S(1)}, bf16[144,1024]{1,0:T(8,128)(2,1)S(1)}, u32[]{:S(2)}, u32[]{:S(2)}) %collective-permute-start.31) | collective-permute-done | bytes 294944 | tf_op jit(solution)/shard_map/ppermute | solution.py:161
  171.9 3.4 %collective-permute-done.29 = bf16[144,2048]{1,0:T(8,128)(2,1)S(1)} collective-permute-done((bf16[144,2048]{1,0:T(8,128)(2,1)S(1)}, bf16[144,2048]{1,0:T(8,128)(2,1)S(1)}, u32[]{:S(2)}, u32[]{:S(2)}) %collective-permute-start.29) | collective-permute-done | bytes 589856 | tf_op jit(solution)/shard_map/ppermute | solution.py:167
  175.7 2.0 %collective-permute-start.32 = (bf16[144,2048]{1,0:T(8,128)(2,1)S(1)}, bf16[144,2048]{1,0:T(8,128)(2,1)S(1)}, u32[]{:S(2)}, u32[]{:S(2)}) collective-permute-start(bf16[144,2048]{1,0:T(8,128)(2,1)S(1)} %pad_maximum_fusion.7), channel_id=1, source_target_pairs={{2,6},{6,4},{4,0},{0,2},{3,7},{7,5},{5,1},{1,3},{10,14},{14,12},{1... | collective-permute-start | bytes 1769480 | tf_op jit(solution)/shard_map/ppermute | solution.py:167
  177.9 0.8 collective-permute-start.33
  178.7 6.0 %collective-permute-done.33 = bf16[144,1024]{1,0:T(8,128)(2,1)S(1)} collective-permute-done((bf16[144,1024]{1,0:T(8,128)(2,1)S(1)}, bf16[144,1024]{1,0:T(8,128)(2,1)S(1)}, u32[]{:S(2)}, u32[]{:S(2)}) %collective-permute-start.33) | collective-permute-done | bytes 294944 | tf_op jit(solution)/shard_map/ppermute | solution.py:161
  184.6 1.9 collective-permute-done.32
  186.8 0.9 pad_maximum_fusion.8
  (88 shorter events, 6.7 us)
Async XLA Ops:
  0.0 5.1 %copy-start.5 = (bf16[144,2048]{1,0:T(8,128)(2,1)S(1)}, bf16[144,2048]{1,0:T(8,128)(2,1)}, u32[]{:S(2)}) copy-start(bf16[144,2048]{1,0:T(8,128)(2,1)} %param.6) | copy-start | bytes 1769476
  0.0 22.5 %collective-permute-start.6 = (bf16[704,2048]{1,0:T(8,128)(2,1)}, bf16[704,2048]{1,0:T(8,128)(2,1)}, u32[]{:S(2)}, u32[]{:S(2)}) collective-permute-start(bf16[704,2048]{1,0:T(8,128)(2,1)} %bitcast.11), channel_id=1, source_target_pairs={{0,1},{1,0},{2,3},{3,2},{4,5},{5,4},{6,7},{7,6},{8,9},{9,8},{10,11... | collective-permute-start | bytes 8650760 | tf_op jit(solution)/shard_map/ppermute | solution.py:161
  1.4 10.2 %collective-permute-start = (bf16[144,1024]{1,0:T(8,128)(2,1)S(1)}, bf16[144,1024]{1,0:T(8,128)(2,1)S(1)}, u32[]{:S(2)}, u32[]{:S(2)}) collective-permute-start(bf16[144,1024]{1,0:T(8,128)(2,1)S(1)} %slice.135), channel_id=1, source_target_pairs={{0,8},{8,0},{1,9},{9,1},{2,10},{10,2},{3,11},{11,3},{4,12},{12,4},... | collective-permute-start | bytes 884744 | tf_op jit(solution)/shard_map/ppermute | solution.py:161
  5.4 17.1 %collective-permute-start.4 = (bf16[144,2176]{1,0:T(8,128)(2,1)S(1)}, bf16[144,2176]{1,0:T(8,128)(2,1)S(1)}, u32[]{:S(2)}, u32[]{:S(2)}) collective-permute-start(bf16[144,2176]{1,0:T(8,128)(2,1)S(1)} %concatenate.50.refs_0_), channel_id=1, source_target_pairs={{2,6},{6,4},{4,0},{0,2},{3,7},{7,5},{5,1},{1,3},{10,14},{14,12},{1... | collective-permute-start | bytes 1880072 | tf_op jit(solution)/shard_map/ppermute | solution.py:167
  7.0 9.6 %collective-permute-start.2 = (bf16[144,1152]{1,0:T(8,128)(2,1)S(1)}, bf16[144,1152]{1,0:T(8,128)(2,1)S(1)}, u32[]{:S(2)}, u32[]{:S(2)}) collective-permute-start(bf16[144,1152]{1,0:T(8,128)(2,1)S(1)} %slice.165), channel_id=1, source_target_pairs={{0,16},{16,0},{1,17},{17,1},{2,18},{18,2},{3,19},{19,3},{4,20},{20... | collective-permute-start | bytes 995336 | tf_op jit(solution)/shard_map/ppermute | solution.py:161
  22.5 3.6 %copy-start = (bf16[144,2176]{1,0:T(8,128)(2,1)}, bf16[144,2176]{1,0:T(8,128)(2,1)S(1)}, u32[]{:S(2)}) copy-start(bf16[144,2176]{1,0:T(8,128)(2,1)S(1)} %collective-permute-done.4.refs_0_) | copy-start | bytes 1880068
  22.5 23.6 %collective-permute-start.7 = (bf16[704,2048]{1,0:T(8,128)(2,1)}, bf16[704,2048]{1,0:T(8,128)(2,1)S(1)}, u32[]{:S(2)}, u32[]{:S(2)}) collective-permute-start(bf16[704,2048]{1,0:T(8,128)(2,1)} %bitcast.16), channel_id=1, source_target_pairs={{0,1},{1,0},{2,3},{3,2},{4,5},{5,4},{6,7},{7,6},{8,9},{9,8},{10,11... | collective-permute-start | bytes 8650760 | tf_op jit(solution)/shard_map/ppermute | solution.py:161
  22.5 23.6 %collective-permute-start.8 = (bf16[704,2048]{1,0:T(8,128)(2,1)}, bf16[704,2048]{1,0:T(8,128)(2,1)S(1)}, u32[]{:S(2)}, u32[]{:S(2)}) collective-permute-start(bf16[704,2048]{1,0:T(8,128)(2,1)} %bitcast.21), channel_id=1, source_target_pairs={{0,1},{1,0},{2,3},{3,2},{4,5},{5,4},{6,7},{7,6},{8,9},{9,8},{10,11... | collective-permute-start | bytes 8650760 | tf_op jit(solution)/shard_map/ppermute | solution.py:161
  23.0 17.0 %collective-permute-start.5 = (bf16[144,2176]{1,0:T(8,128)(2,1)S(1)}, bf16[144,2176]{1,0:T(8,128)(2,1)S(1)}, u32[]{:S(2)}, u32[]{:S(2)}) collective-permute-start(bf16[144,2176]{1,0:T(8,128)(2,1)S(1)} %constant_dynamic-update-slice_fusion), channel_id=1, source_target_pairs={{2,6},{6,4},{4,0},{0,2},{3,7},{7,5},{5,1},{1,3},{10,14},{14,12},{1... | collective-permute-start | bytes 1880072 | tf_op jit(solution)/shard_map/ppermute | solution.py:167
  23.8 22.3 %copy-start.4 = (bf16[4,176,2048]{2,1,0:T(8,128)(2,1)S(1)}, bf16[4,176,2048]{2,1,0:T(8,128)(2,1)}, u32[]{:S(2)}) copy-start(bf16[4,176,2048]{2,1,0:T(8,128)(2,1)} %param.11) | copy-start | bytes 8650756
  23.8 18.1 %collective-permute-start.1 = (bf16[288,1024]{1,0:T(8,128)(2,1)S(1)}, bf16[288,1024]{1,0:T(8,128)(2,1)S(1)}, u32[]{:S(2)}, u32[]{:S(2)}) collective-permute-start(bf16[288,1024]{1,0:T(8,128)(2,1)S(1)} %pad_maximum_fusion.4), channel_id=1, source_target_pairs={{0,16},{16,0},{1,17},{17,1},{2,18},{18,2},{3,19},{19,3},{4,20},{20... | collective-permute-start | bytes 1769480 | tf_op jit(solution)/shard_map/ppermute | solution.py:161
  25.5 17.0 %collective-permute-start.3 = (bf16[288,1152]{1,0:T(8,128)(2,1)S(1)}, bf16[288,1152]{1,0:T(8,128)(2,1)S(1)}, u32[]{:S(2)}, u32[]{:S(2)}) collective-permute-start(bf16[288,1152]{1,0:T(8,128)(2,1)S(1)} %pad_maximum_fusion.2), channel_id=1, source_target_pairs={{0,8},{8,0},{1,9},{9,1},{2,10},{10,2},{3,11},{11,3},{4,12},{12,4},... | collective-permute-start | bytes 1990664 | tf_op jit(solution)/shard_map/ppermute | solution.py:161
  26.1 20.1 %copy-start.3 = (bf16[4,176,2048]{2,1,0:T(8,128)(2,1)S(1)}, bf16[4,176,2048]{2,1,0:T(8,128)(2,1)}, u32[]{:S(2)}) copy-start(bf16[4,176,2048]{2,1,0:T(8,128)(2,1)} %param.10) | copy-start | bytes 8650756
  26.1 15.6 %slice-start = ((bf16[144,2176]{1,0:T(8,128)(2,1)}), bf16[144,1152]{1,0:T(8,128)(2,1)S(1)}, s32[]{:S(2)}) async-start(bf16[144,2176]{1,0:T(8,128)(2,1)} %copy-done), calls=%async_computation | async-start | bytes 663552 | tf_op jit(solution)/shard_map/slice | solution.py:212
  40.1 1.7 copy-start.1
  40.1 20.9 %collective-permute-start.9 = (bf16[288,1024]{1,0:T(8,128)(2,1)S(1)}, bf16[288,1024]{1,0:T(8,128)(2,1)S(1)}, u32[]{:S(2)}, u32[]{:S(2)}) collective-permute-start(bf16[288,1024]{1,0:T(8,128)(2,1)S(1)} %pad_maximum_fusion.5), channel_id=1, source_target_pairs={{0,16},{16,0},{1,17},{17,1},{2,18},{18,2},{3,19},{19,3},{4,20},{20... | collective-permute-start | bytes 1769480 | tf_op jit(solution)/shard_map/ppermute | solution.py:161
  41.7 4.4 %copy-start.2 = (bf16[4,176,2048]{2,1,0:T(8,128)(2,1)S(1)}, bf16[4,176,2048]{2,1,0:T(8,128)(2,1)}, u32[]{:S(2)}) copy-start(bf16[4,176,2048]{2,1,0:T(8,128)(2,1)} %param.9) | copy-start | bytes 8650756
  41.9 19.1 %collective-permute-start.10 = (bf16[288,1152]{1,0:T(8,128)(2,1)S(1)}, bf16[288,1152]{1,0:T(8,128)(2,1)S(1)}, u32[]{:S(2)}, u32[]{:S(2)}) collective-permute-start(bf16[288,1152]{1,0:T(8,128)(2,1)S(1)} %pad_maximum_fusion.3), channel_id=1, source_target_pairs={{0,8},{8,0},{1,9},{9,1},{2,10},{10,2},{3,11},{11,3},{4,12},{12,4},... | collective-permute-start | bytes 1990664 | tf_op jit(solution)/shard_map/ppermute | solution.py:161
  42.5 29.0 %collective-permute-start.13 = (bf16[288,2176]{1,0:T(8,128)(2,1)S(1)}, bf16[288,2176]{1,0:T(8,128)(2,1)S(1)}, u32[]{:S(2)}, u32[]{:S(2)}) collective-permute-start(bf16[288,2176]{1,0:T(8,128)(2,1)S(1)} %pad_maximum_fusion), channel_id=1, source_target_pairs={{2,6},{6,4},{4,0},{0,2},{3,7},{7,5},{5,1},{1,3},{10,14},{14,12},{1... | collective-permute-start | bytes 3760136 | tf_op jit(solution)/shard_map/ppermute | solution.py:167
  61.0 14.4 %collective-permute-start.11 = (bf16[288,1024]{1,0:T(8,128)(2,1)S(1)}, bf16[288,1024]{1,0:T(8,128)(2,1)S(1)}, u32[]{:S(2)}, u32[]{:S(2)}) collective-permute-start(bf16[288,1024]{1,0:T(8,128)(2,1)S(1)} %bitcast.31), channel_id=1, source_target_pairs={{0,16},{16,0},{1,17},{17,1},{2,18},{18,2},{3,19},{19,3},{4,20},{20... | collective-permute-start | bytes 1769480 | tf_op jit(solution)/shard_map/ppermute | solution.py:161
  61.1 14.3 %collective-permute-start.19 = (bf16[288,1024]{1,0:T(8,128)(2,1)S(1)}, bf16[288,1024]{1,0:T(8,128)(2,1)S(1)}, u32[]{:S(2)}, u32[]{:S(2)}) collective-permute-start(bf16[288,1024]{1,0:T(8,128)(2,1)S(1)} %bitcast.29), channel_id=1, source_target_pairs={{0,8},{8,0},{1,9},{9,1},{2,10},{10,2},{3,11},{11,3},{4,12},{12,4},... | collective-permute-start | bytes 1769480 | tf_op jit(solution)/shard_map/ppermute | solution.py:161
  71.6 18.6 %collective-permute-start.17 = (bf16[288,1024]{1,0:T(8,128)(2,1)S(1)}, bf16[288,1024]{1,0:T(8,128)(2,1)S(1)}, u32[]{:S(2)}, u32[]{:S(2)}) collective-permute-start(bf16[288,1024]{1,0:T(8,128)(2,1)S(1)} %concatenate.67), channel_id=1, source_target_pairs={{0,16},{16,0},{1,17},{17,1},{2,18},{18,2},{3,19},{19,3},{4,20},{20... | collective-permute-start | bytes 1769480 | tf_op jit(solution)/shard_map/ppermute | solution.py:161
  72.9 17.3 %collective-permute-start.18 = (bf16[288,1152]{1,0:T(8,128)(2,1)S(1)}, bf16[288,1152]{1,0:T(8,128)(2,1)S(1)}, u32[]{:S(2)}, u32[]{:S(2)}) collective-permute-start(bf16[288,1152]{1,0:T(8,128)(2,1)S(1)} %concatenate.68), channel_id=1, source_target_pairs={{0,8},{8,0},{1,9},{9,1},{2,10},{10,2},{3,11},{11,3},{4,12},{12,4},... | collective-permute-start | bytes 1990664 | tf_op jit(solution)/shard_map/ppermute | solution.py:161
  74.4 27.8 %collective-permute-start.14 = (bf16[288,2176]{1,0:T(8,128)(2,1)S(1)}, bf16[288,2176]{1,0:T(8,128)(2,1)S(1)}, u32[]{:S(2)}, u32[]{:S(2)}) collective-permute-start(bf16[288,2176]{1,0:T(8,128)(2,1)S(1)} %collective-permute-done.13), channel_id=1, source_target_pairs={{2,6},{6,4},{4,0},{0,2},{3,7},{7,5},{5,1},{1,3},{10,14},{14,12},{1... | collective-permute-start | bytes 3760136 | tf_op jit(solution)/shard_map/ppermute | solution.py:167
  90.2 13.6 %collective-permute-start.20 = (bf16[288,1024]{1,0:T(8,128)(2,1)S(1)}, bf16[288,1024]{1,0:T(8,128)(2,1)S(1)}, u32[]{:S(2)}, u32[]{:S(2)}) collective-permute-start(bf16[288,1024]{1,0:T(8,128)(2,1)S(1)} %bitcast.30), channel_id=1, source_target_pairs={{0,16},{16,0},{1,17},{17,1},{2,18},{18,2},{3,19},{19,3},{4,20},{20... | collective-permute-start | bytes 1769480 | tf_op jit(solution)/shard_map/ppermute | solution.py:161
  91.9 12.2 %collective-permute-start.21 = (bf16[288,1024]{1,0:T(8,128)(2,1)S(1)}, bf16[288,1024]{1,0:T(8,128)(2,1)S(1)}, u32[]{:S(2)}, u32[]{:S(2)}) collective-permute-start(bf16[288,1024]{1,0:T(8,128)(2,1)S(1)} %bitcast.28), channel_id=1, source_target_pairs={{0,8},{8,0},{1,9},{9,1},{2,10},{10,2},{3,11},{11,3},{4,12},{12,4},... | collective-permute-start | bytes 1769480 | tf_op jit(solution)/shard_map/ppermute | solution.py:161
  102.3 23.2 %collective-permute-start.15 = (bf16[288,1024]{1,0:T(8,128)(2,1)S(1)}, bf16[288,1024]{1,0:T(8,128)(2,1)S(1)}, u32[]{:S(2)}, u32[]{:S(2)}) collective-permute-start(bf16[288,1024]{1,0:T(8,128)(2,1)S(1)} %concatenate.65), channel_id=1, source_target_pairs={{0,16},{16,0},{1,17},{17,1},{2,18},{18,2},{3,19},{19,3},{4,20},{20... | collective-permute-start | bytes 1769480 | tf_op jit(solution)/shard_map/ppermute | solution.py:161
  103.0 22.5 %collective-permute-start.16 = (bf16[288,1152]{1,0:T(8,128)(2,1)S(1)}, bf16[288,1152]{1,0:T(8,128)(2,1)S(1)}, u32[]{:S(2)}, u32[]{:S(2)}) collective-permute-start(bf16[288,1152]{1,0:T(8,128)(2,1)S(1)} %concatenate.66), channel_id=1, source_target_pairs={{0,8},{8,0},{1,9},{9,1},{2,10},{10,2},{3,11},{11,3},{4,12},{12,4},... | collective-permute-start | bytes 1990664 | tf_op jit(solution)/shard_map/ppermute | solution.py:161
  104.5 40.3 %collective-permute-start.26 = (bf16[288,2048]{1,0:T(8,128)(2,1)S(1)}, bf16[288,2048]{1,0:T(8,128)(2,1)S(1)}, u32[]{:S(2)}, u32[]{:S(2)}) collective-permute-start(bf16[288,2048]{1,0:T(8,128)(2,1)S(1)} %pad_maximum_fusion.1), channel_id=1, source_target_pairs={{2,6},{6,4},{4,0},{0,2},{3,7},{7,5},{5,1},{1,3},{10,14},{14,12},{1... | collective-permute-start | bytes 3538952 | tf_op jit(solution)/shard_map/ppermute | solution.py:167
  125.6 16.8 %collective-permute-start.22 = (bf16[288,1024]{1,0:T(8,128)(2,1)S(1)}, bf16[288,1024]{1,0:T(8,128)(2,1)S(1)}, u32[]{:S(2)}, u32[]{:S(2)}) collective-permute-start(bf16[288,1024]{1,0:T(8,128)(2,1)S(1)} %bitcast.33), channel_id=1, source_target_pairs={{0,16},{16,0},{1,17},{17,1},{2,18},{18,2},{3,19},{19,3},{4,20},{20... | collective-permute-start | bytes 1769480 | tf_op jit(solution)/shard_map/ppermute | solution.py:161
  126.8 15.6 %collective-permute-start.23 = (bf16[288,1024]{1,0:T(8,128)(2,1)S(1)}, bf16[288,1024]{1,0:T(8,128)(2,1)S(1)}, u32[]{:S(2)}, u32[]{:S(2)}) collective-permute-start(bf16[288,1024]{1,0:T(8,128)(2,1)S(1)} %bitcast.32), channel_id=1, source_target_pairs={{0,8},{8,0},{1,9},{9,1},{2,10},{10,2},{3,11},{11,3},{4,12},{12,4},... | collective-permute-start | bytes 1769480 | tf_op jit(solution)/shard_map/ppermute | solution.py:161
  142.4 9.9 %collective-permute-start.24 = (bf16[288,1024]{1,0:T(8,128)(2,1)S(1)}, bf16[288,1024]{1,0:T(8,128)(2,1)S(1)}, u32[]{:S(2)}, u32[]{:S(2)}) collective-permute-start(bf16[288,1024]{1,0:T(8,128)(2,1)S(1)} %bitcast.27), channel_id=1, source_target_pairs={{0,16},{16,0},{1,17},{17,1},{2,18},{18,2},{3,19},{19,3},{4,20},{20... | collective-permute-start | bytes 1769480 | tf_op jit(solution)/shard_map/ppermute | solution.py:161
  143.4 21.6 %collective-permute-start.30 = (bf16[288,1024]{1,0:T(8,128)(2,1)S(1)}, bf16[288,1024]{1,0:T(8,128)(2,1)S(1)}, u32[]{:S(2)}, u32[]{:S(2)}) collective-permute-start(bf16[288,1024]{1,0:T(8,128)(2,1)S(1)} %bitcast.26), channel_id=1, source_target_pairs={{0,8},{8,0},{1,9},{9,1},{2,10},{10,2},{3,11},{11,3},{4,12},{12,4},... | collective-permute-start | bytes 1769480 | tf_op jit(solution)/shard_map/ppermute | solution.py:161
  145.5 11.0 %collective-permute-start.28 = (bf16[144,1024]{1,0:T(8,128)(2,1)S(1)}, bf16[144,1024]{1,0:T(8,128)(2,1)S(1)}, u32[]{:S(2)}, u32[]{:S(2)}) collective-permute-start(bf16[144,1024]{1,0:T(8,128)(2,1)S(1)} %slice.234), channel_id=1, source_target_pairs={{0,16},{16,0},{1,17},{17,1},{2,18},{18,2},{3,19},{19,3},{4,20},{20... | collective-permute-start | bytes 884744 | tf_op jit(solution)/shard_map/ppermute | solution.py:161
  146.7 15.1 %collective-permute-start.27 = (bf16[144,1024]{1,0:T(8,128)(2,1)S(1)}, bf16[144,1024]{1,0:T(8,128)(2,1)S(1)}, u32[]{:S(2)}, u32[]{:S(2)}) collective-permute-start(bf16[144,1024]{1,0:T(8,128)(2,1)S(1)} %slice.235), channel_id=1, source_target_pairs={{0,8},{8,0},{1,9},{9,1},{2,10},{10,2},{3,11},{11,3},{4,12},{12,4},... | collective-permute-start | bytes 884744 | tf_op jit(solution)/shard_map/ppermute | solution.py:161
  152.6 15.1 %collective-permute-start.25 = (bf16[144,1024]{1,0:T(8,128)(2,1)S(1)}, bf16[144,1024]{1,0:T(8,128)(2,1)S(1)}, u32[]{:S(2)}, u32[]{:S(2)}) collective-permute-start(bf16[144,1024]{1,0:T(8,128)(2,1)S(1)} %slice.236), channel_id=1, source_target_pairs={{0,8},{8,0},{1,9},{9,1},{2,10},{10,2},{3,11},{11,3},{4,12},{12,4},... | collective-permute-start | bytes 884744 | tf_op jit(solution)/shard_map/ppermute | solution.py:161
  161.9 13.4 %collective-permute-start.29 = (bf16[144,2048]{1,0:T(8,128)(2,1)S(1)}, bf16[144,2048]{1,0:T(8,128)(2,1)S(1)}, u32[]{:S(2)}, u32[]{:S(2)}) collective-permute-start(bf16[144,2048]{1,0:T(8,128)(2,1)S(1)} %pad_maximum_fusion.6), channel_id=1, source_target_pairs={{2,6},{6,4},{4,0},{0,2},{3,7},{7,5},{5,1},{1,3},{10,14},{14,12},{1... | collective-permute-start | bytes 1769480 | tf_op jit(solution)/shard_map/ppermute | solution.py:167
  165.1 6.8 %collective-permute-start.31 = (bf16[144,1024]{1,0:T(8,128)(2,1)S(1)}, bf16[144,1024]{1,0:T(8,128)(2,1)S(1)}, u32[]{:S(2)}, u32[]{:S(2)}) collective-permute-start(bf16[144,1024]{1,0:T(8,128)(2,1)S(1)} %slice.233), channel_id=1, source_target_pairs={{0,16},{16,0},{1,17},{17,1},{2,18},{18,2},{3,19},{19,3},{4,20},{20... | collective-permute-start | bytes 884744 | tf_op jit(solution)/shard_map/ppermute | solution.py:161
  167.1 11.6 %collective-permute-start.12 = (bf16[144,1024]{1,0:T(8,128)(2,1)S(1)}, bf16[144,1024]{1,0:T(8,128)(2,1)S(1)}, u32[]{:S(2)}, u32[]{:S(2)}) collective-permute-start(bf16[144,1024]{1,0:T(8,128)(2,1)S(1)} %slice.237), channel_id=1, source_target_pairs={{0,8},{8,0},{1,9},{9,1},{2,10},{10,2},{3,11},{11,3},{4,12},{12,4},... | collective-permute-start | bytes 884744 | tf_op jit(solution)/shard_map/ppermute | solution.py:161
  175.7 10.8 %collective-permute-start.32 = (bf16[144,2048]{1,0:T(8,128)(2,1)S(1)}, bf16[144,2048]{1,0:T(8,128)(2,1)S(1)}, u32[]{:S(2)}, u32[]{:S(2)}) collective-permute-start(bf16[144,2048]{1,0:T(8,128)(2,1)S(1)} %pad_maximum_fusion.7), channel_id=1, source_target_pairs={{2,6},{6,4},{4,0},{0,2},{3,7},{7,5},{5,1},{1,3},{10,14},{14,12},{1... | collective-permute-start | bytes 1769480 | tf_op jit(solution)/shard_map/ppermute | solution.py:167
  177.9 6.8 %collective-permute-start.33 = (bf16[144,1024]{1,0:T(8,128)(2,1)S(1)}, bf16[144,1024]{1,0:T(8,128)(2,1)S(1)}, u32[]{:S(2)}, u32[]{:S(2)}) collective-permute-start(bf16[144,1024]{1,0:T(8,128)(2,1)S(1)} %slice.232), channel_id=1, source_target_pairs={{0,16},{16,0},{1,17},{17,1},{2,18},{18,2},{3,19},{19,3},{4,20},{20... | collective-permute-start | bytes 884744 | tf_op jit(solution)/shard_map/ppermute | solution.py:161
where the time goes:
time: 188 us
  waiting for transfers between devices  75.5 us (40%)
  Pallas kernels  59.4 us (32%)
  starting transfers between devices  45.5 us (24%)
  other arithmetic  4.42 us (2%)
  local copies, waits for them, and re-layouts  2.3 us (1%)
    pallas_call x4, Pallas kernels, ffn(): pl.pallas_call(functools.partial(ffn_kernel, ny, nx, experts, per_group),...  59.4 us
    ppermute x7, waiting for transfers between devices, ring_step(): lax.ppermute(value, 'line', [(order[i], order[(i + 1) % n]) for i in rang...  44.4 us
    ppermute x27, waiting for transfers between devices, shift(): return lax.ppermute(value, axis, [(i, (i + by) % n) for i in range(n)])  31.1 us
    ppermute x27, starting transfers between devices, shift(): return lax.ppermute(value, axis, [(i, (i + by) % n) for i in range(n)])  27.5 us
    ppermute x7, starting transfers between devices, ring_step(): lax.ppermute(value, 'line', [(order[i], order[(i + 1) % n]) for i in rang...  18 us
  transfers between devices with their start and end apart: 34, of which 15 were waited for; matrix products, arithmetic and copies ran while one was open for 3% of the time, Pallas kernels for 32%

commit v1 on v0

--- a/solution.py
+++ b/solution.py
@@ -98,7 +98,7 @@
             for h in range(2)
         )
 
-    @pl.loop(0, half // TILE)
+    @pl.loop(0, half // TILE, unroll=2)
     def _(step):
         part = down_product(step * TILE)
         to = pl.ds(pl.multiple_of(step * TILE, TILE), TILE)
@@ -109,7 +109,7 @@
             else:
                 keep_a[:, to] = block
 
-    @pl.loop(0, half // TILE)
+    @pl.loop(0, half // TILE, unroll=2)
     def _(step):
         part = down_product(half + step * TILE)
         to = pl.ds(pl.multiple_of(step * TILE, TILE), TILE)

time: 188 us -> 187 us (level)
  Pallas kernels: 59.4 us -> 56.8 us
    pallas_call x4, Pallas kernels: 59.4 us -> 56.8 us  [ffn(): pl.pallas_call(functools.partial(ffn_kernel, ny, nx, experts, per_group),...]
    ppermute x7, waiting for transfers between devices: 44.4 us -> 46.7 us  [ring_step(): lax.ppermute(value, 'line', [(order[i], order[(i + 1) % n]) for i in rang...]
  transfers between devices with their start and end apart: 34 -> 34, of which waited for: 15 -> 13; matrix products, arithmetic and copies ran while one was open for 3% -> 3% of each run, Pallas kernels for 32% -> 30%
where the time goes in v1:
time: 187 us
  waiting for transfers between devices  76.7 us (41%)
  Pallas kernels  56.8 us (30%)
  starting transfers between devices  46.2 us (25%)
  other arithmetic  4.42 us (2%)
  local copies, waits for them, and re-layouts  2.3 us (1%)
    pallas_call x4, Pallas kernels, ffn(): pl.pallas_call(functools.partial(ffn_kernel, ny, nx, experts, per_group),...  56.8 us
    ppermute x7, waiting for transfers between devices, ring_step(): lax.ppermute(value, 'line', [(order[i], order[(i + 1) % n]) for i in rang...  46.7 us
    ppermute x27, waiting for transfers between devices, shift(): return lax.ppermute(value, axis, [(i, (i + by) % n) for i in range(n)])  30.1 us
    ppermute x27, starting transfers between devices, shift(): return lax.ppermute(value, axis, [(i, (i + by) % n) for i in range(n)])  28 us
    ppermute x7, starting transfers between devices, ring_step(): lax.ppermute(value, 'line', [(order[i], order[(i + 1) % n]) for i in rang...  18.1 us
  transfers between devices with their start and end apart: 34, of which 13 were waited for; matrix products, arithmetic and copies ran while one was open for 3% of the time, Pallas kernels for 30%

profile of v1, /device:TPU:0, one launch (start us, length us, event | category | flops | bytes accessed | tf_op | source)
XLA Modules:
  0.0 186.9 jit_solution(2935631710745037237)
XLA Ops:
  0.5 1.0 slice.135
  1.4 2.6 %collective-permute-start = (bf16[144,1024]{1,0:T(8,128)(2,1)S(1)}, bf16[144,1024]{1,0:T(8,128)(2,1)S(1)}, u32[]{:S(2)}, u32[]{:S(2)}) collective-permute-start(bf16[144,1024]{1,0:T(8,128)(2,1)S(1)} %slice.135), channel_id=1, source_target_pairs={{0,8},{8,0},{1,9},{9,1},{2,10},{10,2},{3,11},{11,3},{4,12},{12,4},... | collective-permute-start | bytes 884744 | tf_op jit(solution)/shard_map/ppermute | solution.py:161
  4.1 0.7 select_reduce_fusion
  5.4 1.6 collective-permute-start.4
  7.0 1.6 collective-permute-start.2
  8.6 3.1 %collective-permute-done.refs_1_ = bf16[144,1024]{1,0:T(8,128)(2,1)S(1)} collective-permute-done((bf16[144,1024]{1,0:T(8,128)(2,1)S(1)}, bf16[144,1024]{1,0:T(8,128)(2,1)S(1)}, u32[]{:S(2)}, u32[]{:S(2)}) %collective-permute-start) | collective-permute-done | bytes 294944 | tf_op jit(solution)/shard_map/ppermute | solution.py:161
  11.7 5.0 %collective-permute-done.2.refs_2_ = bf16[144,1152]{1,0:T(8,128)(2,1)S(1)} collective-permute-done((bf16[144,1152]{1,0:T(8,128)(2,1)S(1)}, bf16[144,1152]{1,0:T(8,128)(2,1)S(1)}, u32[]{:S(2)}, u32[]{:S(2)}) %collective-permute-start.2) | collective-permute-done | bytes 331808 | tf_op jit(solution)/shard_map/ppermute | solution.py:161
  16.7 5.8 %collective-permute-done.4.refs_0_ = bf16[144,2176]{1,0:T(8,128)(2,1)S(1)} collective-permute-done((bf16[144,2176]{1,0:T(8,128)(2,1)S(1)}, bf16[144,2176]{1,0:T(8,128)(2,1)S(1)}, u32[]{:S(2)}, u32[]{:S(2)}) %collective-permute-start.4) | collective-permute-done | bytes 626720 | tf_op jit(solution)/shard_map/ppermute | solution.py:167
  23.0 0.8 collective-permute-start.5
  23.8 1.6 collective-permute-start.1
  25.5 0.6 collective-permute-start.3
  26.1 13.9 %collective-permute-done.5 = bf16[144,2176]{1,0:T(8,128)(2,1)S(1)} collective-permute-done((bf16[144,2176]{1,0:T(8,128)(2,1)S(1)}, bf16[144,2176]{1,0:T(8,128)(2,1)S(1)}, u32[]{:S(2)}, u32[]{:S(2)}) %collective-permute-start.5) | collective-permute-done | bytes 626720 | tf_op jit(solution)/shard_map/ppermute | solution.py:167
  40.1 1.6 collective-permute-start.9
  41.9 0.6 collective-permute-start.10
  42.5 3.6 %collective-permute-start.13 = (bf16[288,2176]{1,0:T(8,128)(2,1)S(1)}, bf16[288,2176]{1,0:T(8,128)(2,1)S(1)}, u32[]{:S(2)}, u32[]{:S(2)}) collective-permute-start(bf16[288,2176]{1,0:T(8,128)(2,1)S(1)} %pad_maximum_fusion), channel_id=1, source_target_pairs={{2,6},{6,4},{4,0},{0,2},{3,7},{7,5},{5,1},{1,3},{10,14},{14,12},{1... | collective-permute-start | bytes 3760136 | tf_op jit(solution)/shard_map/ppermute | solution.py:167
  46.2 14.1 %shard_map.64 = (bf16[1,288,1024]{2,1,0:T(8,128)(2,1)S(1)}, f32[288,1024]{1,0:T(8,128)S(1)}, bf16[1,288,1024]{2,1,0:T(8,128)(2,1)S(1)}, f32[288,1024]{1,0:T(8,128)S(1)}) custom-call(bf16[144,2176]{1,0:T(8,128)(2,1)S(1)} %concatenate.50.refs_0_, bf16[144,1024]{1,0:T(8,128)(2,1)S(1)} %collective-permute-done.refs_1_, ...), custom_call_target="tpu_custom_call" | custom-call | flops 9965666304 | bytes 9437184 | tf_op jit(solution)/shard_map/pallas_call | solution.py:135
  60.4 0.6 collective-permute-start.19
  61.0 10.5 %collective-permute-done.13 = bf16[288,2176]{1,0:T(8,128)(2,1)S(1)} collective-permute-done((bf16[288,2176]{1,0:T(8,128)(2,1)S(1)}, bf16[288,2176]{1,0:T(8,128)(2,1)S(1)}, u32[]{:S(2)}, u32[]{:S(2)}) %collective-permute-start.13) | collective-permute-done | bytes 1253408 | tf_op jit(solution)/shard_map/ppermute | solution.py:167
  71.6 1.2 collective-permute-start.17
  72.9 1.6 collective-permute-start.18
  74.4 0.8 collective-permute-start.14
  75.3 14.1 %shard_map.65 = (bf16[1,288,1024]{2,1,0:T(8,128)(2,1)S(1)}, f32[288,1024]{1,0:T(8,128)S(1)}, bf16[1,288,1024]{2,1,0:T(8,128)(2,1)S(1)}, f32[288,1024]{1,0:T(8,128)S(1)}) custom-call(bf16[144,2176]{1,0:T(8,128)(2,1)S(1)} %copy-done.1, bf16[144,1024]{1,0:T(8,128)(2,1)S(1)} %slice.167.refs_1_, bf16[144,1152]{1,0:T(8,128)(2,1)S(1)} %slice.169.refs_2_, ...), custom_call_target="tpu_custom_call" | custom-call | flops 9965666304 | bytes 9437184 | tf_op jit(solution)/shard_map/pallas_call | solution.py:135
  89.5 1.0 collective-permute-start.20
  90.4 1.5 collective-permute-start.21
  92.0 10.3 %collective-permute-done.14 = bf16[288,2176]{1,0:T(8,128)(2,1)S(1)} collective-permute-done((bf16[288,2176]{1,0:T(8,128)(2,1)S(1)}, bf16[288,2176]{1,0:T(8,128)(2,1)S(1)}, u32[]{:S(2)}, u32[]{:S(2)}) %collective-permute-start.14) | collective-permute-done | bytes 1253408 | tf_op jit(solution)/shard_map/ppermute | solution.py:167
  102.3 0.7 collective-permute-start.15
  103.0 0.6 collective-permute-start.16
  104.2 5.2 %collective-permute-start.26 = (bf16[288,2048]{1,0:T(8,128)(2,1)S(1)}, bf16[288,2048]{1,0:T(8,128)(2,1)S(1)}, u32[]{:S(2)}, u32[]{:S(2)}) collective-permute-start(bf16[288,2048]{1,0:T(8,128)(2,1)S(1)} %pad_maximum_fusion.1), channel_id=1, source_target_pairs={{2,6},{6,4},{4,0},{0,2},{3,7},{7,5},{5,1},{1,3},{10,14},{14,12},{1... | collective-permute-start | bytes 3538952 | tf_op jit(solution)/shard_map/ppermute | solution.py:167
  109.5 14.1 %shard_map.66 = (bf16[1,288,1024]{2,1,0:T(8,128)(2,1)S(1)}, f32[288,1024]{1,0:T(8,128)S(1)}, bf16[1,288,1024]{2,1,0:T(8,128)(2,1)S(1)}, f32[288,1024]{1,0:T(8,128)S(1)}) custom-call(bf16[144,2176]{1,0:T(8,128)(2,1)S(1)} %slice.173.refs_0_, bf16[144,1024]{1,0:T(8,128)(2,1)S(1)} %slice.174.refs_1_, bf16[144,1152]{1,0:T(8,128)(2,1)S(1)} %slice.175.refs_2_, ...), custom_call_target="tpu_custom_call" | custom-call | flops 9965666304 | bytes 9437184 | tf_op jit(solution)/shard_map/pallas_call | solution.py:135
  123.6 1.2 collective-permute-start.22
  125.4 14.4 %shard_map.67 = (bf16[1,288,1024]{2,1,0:T(8,128)(2,1)S(1)}, f32[288,1024]{1,0:T(8,128)S(1)}, bf16[1,288,1024]{2,1,0:T(8,128)(2,1)S(1)}, f32[288,1024]{1,0:T(8,128)S(1)}) custom-call(bf16[144,2176]{1,0:T(8,128)(2,1)S(1)} %slice.172.refs_0_, bf16[144,1024]{1,0:T(8,128)(2,1)S(1)} %slice.176.refs_1_, bf16[144,1152]{1,0:T(8,128)(2,1)S(1)} %slice.177.refs_2_, ...), custom_call_target="tpu_custom_call" | custom-call | flops 9965666304 | bytes 9437184 | tf_op jit(solution)/shard_map/pallas_call | solution.py:135
  139.8 0.9 collective-permute-start.24
  140.7 1.5 collective-permute-start.30
  142.8 1.2 collective-permute-start.28
  144.7 5.9 %collective-permute-done.24 = bf16[288,1024]{1,0:T(8,128)(2,1)S(1)} collective-permute-done((bf16[288,1024]{1,0:T(8,128)(2,1)S(1)}, bf16[288,1024]{1,0:T(8,128)(2,1)S(1)}, u32[]{:S(2)}, u32[]{:S(2)}) %collective-permute-start.24) | collective-permute-done | bytes 589856 | tf_op jit(solution)/shard_map/ppermute | solution.py:161
  150.8 1.6 collective-permute-start.25
  152.4 1.3 collective-permute-done.28
  153.8 5.2 %collective-permute-done.27 = bf16[144,1024]{1,0:T(8,128)(2,1)S(1)} collective-permute-done((bf16[144,1024]{1,0:T(8,128)(2,1)S(1)}, bf16[144,1024]{1,0:T(8,128)(2,1)S(1)}, u32[]{:S(2)}, u32[]{:S(2)}) %collective-permute-start.27) | collective-permute-done | bytes 294944 | tf_op jit(solution)/shard_map/ppermute | solution.py:161
  159.1 4.4 %collective-permute-start.29 = (bf16[144,2048]{1,0:T(8,128)(2,1)S(1)}, bf16[144,2048]{1,0:T(8,128)(2,1)S(1)}, u32[]{:S(2)}, u32[]{:S(2)}) collective-permute-start(bf16[144,2048]{1,0:T(8,128)(2,1)S(1)} %pad_maximum_fusion.6), channel_id=1, source_target_pairs={{2,6},{6,4},{4,0},{0,2},{3,7},{7,5},{5,1},{1,3},{10,14},{14,12},{1... | collective-permute-start | bytes 1769480 | tf_op jit(solution)/shard_map/ppermute | solution.py:167
  163.8 1.6 collective-permute-start.31
  165.6 0.8 collective-permute-start.12
  166.4 4.2 %collective-permute-done.31 = bf16[144,1024]{1,0:T(8,128)(2,1)S(1)} collective-permute-done((bf16[144,1024]{1,0:T(8,128)(2,1)S(1)}, bf16[144,1024]{1,0:T(8,128)(2,1)S(1)}, u32[]{:S(2)}, u32[]{:S(2)}) %collective-permute-start.31) | collective-permute-done | bytes 294944 | tf_op jit(solution)/shard_map/ppermute | solution.py:161
  170.6 4.0 %collective-permute-done.29 = bf16[144,2048]{1,0:T(8,128)(2,1)S(1)} collective-permute-done((bf16[144,2048]{1,0:T(8,128)(2,1)S(1)}, bf16[144,2048]{1,0:T(8,128)(2,1)S(1)}, u32[]{:S(2)}, u32[]{:S(2)}) %collective-permute-start.29) | collective-permute-done | bytes 589856 | tf_op jit(solution)/shard_map/ppermute | solution.py:167
  174.9 1.6 collective-permute-start.32
  176.8 1.4 collective-permute-start.33
  178.2 5.3 %collective-permute-done.33 = bf16[144,1024]{1,0:T(8,128)(2,1)S(1)} collective-permute-done((bf16[144,1024]{1,0:T(8,128)(2,1)S(1)}, bf16[144,1024]{1,0:T(8,128)(2,1)S(1)}, u32[]{:S(2)}, u32[]{:S(2)}) %collective-permute-start.33) | collective-permute-done | bytes 294944 | tf_op jit(solution)/shard_map/ppermute | solution.py:161
  183.6 2.2 %collective-permute-done.32 = bf16[144,2048]{1,0:T(8,128)(2,1)S(1)} collective-permute-done((bf16[144,2048]{1,0:T(8,128)(2,1)S(1)}, bf16[144,2048]{1,0:T(8,128)(2,1)S(1)}, u32[]{:S(2)}, u32[]{:S(2)}) %collective-permute-start.32) | collective-permute-done | bytes 589856 | tf_op jit(solution)/shard_map/ppermute | solution.py:167
  186.1 0.9 pad_maximum_fusion.8
  (88 shorter events, 6.3 us)
Async XLA Ops:
  0.0 5.1 %copy-start.5 = (bf16[144,2048]{1,0:T(8,128)(2,1)S(1)}, bf16[144,2048]{1,0:T(8,128)(2,1)}, u32[]{:S(2)}) copy-start(bf16[144,2048]{1,0:T(8,128)(2,1)} %param.6) | copy-start | bytes 1769476
  0.0 22.5 %collective-permute-start.6 = (bf16[704,2048]{1,0:T(8,128)(2,1)}, bf16[704,2048]{1,0:T(8,128)(2,1)}, u32[]{:S(2)}, u32[]{:S(2)}) collective-permute-start(bf16[704,2048]{1,0:T(8,128)(2,1)} %bitcast.11), channel_id=1, source_target_pairs={{0,1},{1,0},{2,3},{3,2},{4,5},{5,4},{6,7},{7,6},{8,9},{9,8},{10,11... | collective-permute-start | bytes 8650760 | tf_op jit(solution)/shard_map/ppermute | solution.py:161
  1.4 10.2 %collective-permute-start = (bf16[144,1024]{1,0:T(8,128)(2,1)S(1)}, bf16[144,1024]{1,0:T(8,128)(2,1)S(1)}, u32[]{:S(2)}, u32[]{:S(2)}) collective-permute-start(bf16[144,1024]{1,0:T(8,128)(2,1)S(1)} %slice.135), channel_id=1, source_target_pairs={{0,8},{8,0},{1,9},{9,1},{2,10},{10,2},{3,11},{11,3},{4,12},{12,4},... | collective-permute-start | bytes 884744 | tf_op jit(solution)/shard_map/ppermute | solution.py:161
  5.4 17.1 %collective-permute-start.4 = (bf16[144,2176]{1,0:T(8,128)(2,1)S(1)}, bf16[144,2176]{1,0:T(8,128)(2,1)S(1)}, u32[]{:S(2)}, u32[]{:S(2)}) collective-permute-start(bf16[144,2176]{1,0:T(8,128)(2,1)S(1)} %concatenate.50.refs_0_), channel_id=1, source_target_pairs={{2,6},{6,4},{4,0},{0,2},{3,7},{7,5},{5,1},{1,3},{10,14},{14,12},{1... | collective-permute-start | bytes 1880072 | tf_op jit(solution)/shard_map/ppermute | solution.py:167
  7.0 9.6 %collective-permute-start.2 = (bf16[144,1152]{1,0:T(8,128)(2,1)S(1)}, bf16[144,1152]{1,0:T(8,128)(2,1)S(1)}, u32[]{:S(2)}, u32[]{:S(2)}) collective-permute-start(bf16[144,1152]{1,0:T(8,128)(2,1)S(1)} %slice.165), channel_id=1, source_target_pairs={{0,16},{16,0},{1,17},{17,1},{2,18},{18,2},{3,19},{19,3},{4,20},{20... | collective-permute-start | bytes 995336 | tf_op jit(solution)/shard_map/ppermute | solution.py:161
  22.5 3.6 %copy-start = (bf16[144,2176]{1,0:T(8,128)(2,1)}, bf16[144,2176]{1,0:T(8,128)(2,1)S(1)}, u32[]{:S(2)}) copy-start(bf16[144,2176]{1,0:T(8,128)(2,1)S(1)} %collective-permute-done.4.refs_0_) | copy-start | bytes 1880068
  22.5 23.6 %collective-permute-start.7 = (bf16[704,2048]{1,0:T(8,128)(2,1)}, bf16[704,2048]{1,0:T(8,128)(2,1)S(1)}, u32[]{:S(2)}, u32[]{:S(2)}) collective-permute-start(bf16[704,2048]{1,0:T(8,128)(2,1)} %bitcast.16), channel_id=1, source_target_pairs={{0,1},{1,0},{2,3},{3,2},{4,5},{5,4},{6,7},{7,6},{8,9},{9,8},{10,11... | collective-permute-start | bytes 8650760 | tf_op jit(solution)/shard_map/ppermute | solution.py:161
  22.5 23.6 %collective-permute-start.8 = (bf16[704,2048]{1,0:T(8,128)(2,1)}, bf16[704,2048]{1,0:T(8,128)(2,1)S(1)}, u32[]{:S(2)}, u32[]{:S(2)}) collective-permute-start(bf16[704,2048]{1,0:T(8,128)(2,1)} %bitcast.21), channel_id=1, source_target_pairs={{0,1},{1,0},{2,3},{3,2},{4,5},{5,4},{6,7},{7,6},{8,9},{9,8},{10,11... | collective-permute-start | bytes 8650760 | tf_op jit(solution)/shard_map/ppermute | solution.py:161
  23.0 17.0 %collective-permute-start.5 = (bf16[144,2176]{1,0:T(8,128)(2,1)S(1)}, bf16[144,2176]{1,0:T(8,128)(2,1)S(1)}, u32[]{:S(2)}, u32[]{:S(2)}) collective-permute-start(bf16[144,2176]{1,0:T(8,128)(2,1)S(1)} %constant_dynamic-update-slice_fusion), channel_id=1, source_target_pairs={{2,6},{6,4},{4,0},{0,2},{3,7},{7,5},{5,1},{1,3},{10,14},{14,12},{1... | collective-permute-start | bytes 1880072 | tf_op jit(solution)/shard_map/ppermute | solution.py:167
  23.8 22.3 %copy-start.4 = (bf16[4,176,2048]{2,1,0:T(8,128)(2,1)S(1)}, bf16[4,176,2048]{2,1,0:T(8,128)(2,1)}, u32[]{:S(2)}) copy-start(bf16[4,176,2048]{2,1,0:T(8,128)(2,1)} %param.11) | copy-start | bytes 8650756
  23.8 18.1 %collective-permute-start.1 = (bf16[288,1024]{1,0:T(8,128)(2,1)S(1)}, bf16[288,1024]{1,0:T(8,128)(2,1)S(1)}, u32[]{:S(2)}, u32[]{:S(2)}) collective-permute-start(bf16[288,1024]{1,0:T(8,128)(2,1)S(1)} %pad_maximum_fusion.4), channel_id=1, source_target_pairs={{0,16},{16,0},{1,17},{17,1},{2,18},{18,2},{3,19},{19,3},{4,20},{20... | collective-permute-start | bytes 1769480 | tf_op jit(solution)/shard_map/ppermute | solution.py:161
  25.5 17.0 %collective-permute-start.3 = (bf16[288,1152]{1,0:T(8,128)(2,1)S(1)}, bf16[288,1152]{1,0:T(8,128)(2,1)S(1)}, u32[]{:S(2)}, u32[]{:S(2)}) collective-permute-start(bf16[288,1152]{1,0:T(8,128)(2,1)S(1)} %pad_maximum_fusion.2), channel_id=1, source_target_pairs={{0,8},{8,0},{1,9},{9,1},{2,10},{10,2},{3,11},{11,3},{4,12},{12,4},... | collective-permute-start | bytes 1990664 | tf_op jit(solution)/shard_map/ppermute | solution.py:161
  26.1 20.1 %copy-start.3 = (bf16[4,176,2048]{2,1,0:T(8,128)(2,1)S(1)}, bf16[4,176,2048]{2,1,0:T(8,128)(2,1)}, u32[]{:S(2)}) copy-start(bf16[4,176,2048]{2,1,0:T(8,128)(2,1)} %param.10) | copy-start | bytes 8650756
  26.1 15.6 %slice-start = ((bf16[144,2176]{1,0:T(8,128)(2,1)}), bf16[144,1152]{1,0:T(8,128)(2,1)S(1)}, s32[]{:S(2)}) async-start(bf16[144,2176]{1,0:T(8,128)(2,1)} %copy-done), calls=%async_computation | async-start | bytes 663552 | tf_op jit(solution)/shard_map/slice | solution.py:212
  40.1 1.7 copy-start.1
  40.1 20.2 %collective-permute-start.9 = (bf16[288,1024]{1,0:T(8,128)(2,1)S(1)}, bf16[288,1024]{1,0:T(8,128)(2,1)S(1)}, u32[]{:S(2)}, u32[]{:S(2)}) collective-permute-start(bf16[288,1024]{1,0:T(8,128)(2,1)S(1)} %pad_maximum_fusion.5), channel_id=1, source_target_pairs={{0,16},{16,0},{1,17},{17,1},{2,18},{18,2},{3,19},{19,3},{4,20},{20... | collective-permute-start | bytes 1769480 | tf_op jit(solution)/shard_map/ppermute | solution.py:161
  41.7 4.4 %copy-start.2 = (bf16[4,176,2048]{2,1,0:T(8,128)(2,1)S(1)}, bf16[4,176,2048]{2,1,0:T(8,128)(2,1)}, u32[]{:S(2)}) copy-start(bf16[4,176,2048]{2,1,0:T(8,128)(2,1)} %param.9) | copy-start | bytes 8650756
  41.9 18.4 %collective-permute-start.10 = (bf16[288,1152]{1,0:T(8,128)(2,1)S(1)}, bf16[288,1152]{1,0:T(8,128)(2,1)S(1)}, u32[]{:S(2)}, u32[]{:S(2)}) collective-permute-start(bf16[288,1152]{1,0:T(8,128)(2,1)S(1)} %pad_maximum_fusion.3), channel_id=1, source_target_pairs={{0,8},{8,0},{1,9},{9,1},{2,10},{10,2},{3,11},{11,3},{4,12},{12,4},... | collective-permute-start | bytes 1990664 | tf_op jit(solution)/shard_map/ppermute | solution.py:161
  42.5 29.0 %collective-permute-start.13 = (bf16[288,2176]{1,0:T(8,128)(2,1)S(1)}, bf16[288,2176]{1,0:T(8,128)(2,1)S(1)}, u32[]{:S(2)}, u32[]{:S(2)}) collective-permute-start(bf16[288,2176]{1,0:T(8,128)(2,1)S(1)} %pad_maximum_fusion), channel_id=1, source_target_pairs={{2,6},{6,4},{4,0},{0,2},{3,7},{7,5},{5,1},{1,3},{10,14},{14,12},{1... | collective-permute-start | bytes 3760136 | tf_op jit(solution)/shard_map/ppermute | solution.py:167
  60.3 14.9 %collective-permute-start.11 = (bf16[288,1024]{1,0:T(8,128)(2,1)S(1)}, bf16[288,1024]{1,0:T(8,128)(2,1)S(1)}, u32[]{:S(2)}, u32[]{:S(2)}) collective-permute-start(bf16[288,1024]{1,0:T(8,128)(2,1)S(1)} %bitcast.31), channel_id=1, source_target_pairs={{0,16},{16,0},{1,17},{17,1},{2,18},{18,2},{3,19},{19,3},{4,20},{20... | collective-permute-start | bytes 1769480 | tf_op jit(solution)/shard_map/ppermute | solution.py:161
  60.4 14.9 %collective-permute-start.19 = (bf16[288,1024]{1,0:T(8,128)(2,1)S(1)}, bf16[288,1024]{1,0:T(8,128)(2,1)S(1)}, u32[]{:S(2)}, u32[]{:S(2)}) collective-permute-start(bf16[288,1024]{1,0:T(8,128)(2,1)S(1)} %bitcast.29), channel_id=1, source_target_pairs={{0,8},{8,0},{1,9},{9,1},{2,10},{10,2},{3,11},{11,3},{4,12},{12,4},... | collective-permute-start | bytes 1769480 | tf_op jit(solution)/shard_map/ppermute | solution.py:161
  71.6 17.8 %collective-permute-start.17 = (bf16[288,1024]{1,0:T(8,128)(2,1)S(1)}, bf16[288,1024]{1,0:T(8,128)(2,1)S(1)}, u32[]{:S(2)}, u32[]{:S(2)}) collective-permute-start(bf16[288,1024]{1,0:T(8,128)(2,1)S(1)} %concatenate.67), channel_id=1, source_target_pairs={{0,16},{16,0},{1,17},{17,1},{2,18},{18,2},{3,19},{19,3},{4,20},{20... | collective-permute-start | bytes 1769480 | tf_op jit(solution)/shard_map/ppermute | solution.py:161
  72.9 16.6 %collective-permute-start.18 = (bf16[288,1152]{1,0:T(8,128)(2,1)S(1)}, bf16[288,1152]{1,0:T(8,128)(2,1)S(1)}, u32[]{:S(2)}, u32[]{:S(2)}) collective-permute-start(bf16[288,1152]{1,0:T(8,128)(2,1)S(1)} %concatenate.68), channel_id=1, source_target_pairs={{0,8},{8,0},{1,9},{9,1},{2,10},{10,2},{3,11},{11,3},{4,12},{12,4},... | collective-permute-start | bytes 1990664 | tf_op jit(solution)/shard_map/ppermute | solution.py:161
  74.4 27.8 %collective-permute-start.14 = (bf16[288,2176]{1,0:T(8,128)(2,1)S(1)}, bf16[288,2176]{1,0:T(8,128)(2,1)S(1)}, u32[]{:S(2)}, u32[]{:S(2)}) collective-permute-start(bf16[288,2176]{1,0:T(8,128)(2,1)S(1)} %collective-permute-done.13), channel_id=1, source_target_pairs={{2,6},{6,4},{4,0},{0,2},{3,7},{7,5},{5,1},{1,3},{10,14},{14,12},{1... | collective-permute-start | bytes 3760136 | tf_op jit(solution)/shard_map/ppermute | solution.py:167
  89.5 14.3 %collective-permute-start.20 = (bf16[288,1024]{1,0:T(8,128)(2,1)S(1)}, bf16[288,1024]{1,0:T(8,128)(2,1)S(1)}, u32[]{:S(2)}, u32[]{:S(2)}) collective-permute-start(bf16[288,1024]{1,0:T(8,128)(2,1)S(1)} %bitcast.30), channel_id=1, source_target_pairs={{0,16},{16,0},{1,17},{17,1},{2,18},{18,2},{3,19},{19,3},{4,20},{20... | collective-permute-start | bytes 1769480 | tf_op jit(solution)/shard_map/ppermute | solution.py:161
  90.4 13.3 %collective-permute-start.21 = (bf16[288,1024]{1,0:T(8,128)(2,1)S(1)}, bf16[288,1024]{1,0:T(8,128)(2,1)S(1)}, u32[]{:S(2)}, u32[]{:S(2)}) collective-permute-start(bf16[288,1024]{1,0:T(8,128)(2,1)S(1)} %bitcast.28), channel_id=1, source_target_pairs={{0,8},{8,0},{1,9},{9,1},{2,10},{10,2},{3,11},{11,3},{4,12},{12,4},... | collective-permute-start | bytes 1769480 | tf_op jit(solution)/shard_map/ppermute | solution.py:161
  102.3 21.3 %collective-permute-start.15 = (bf16[288,1024]{1,0:T(8,128)(2,1)S(1)}, bf16[288,1024]{1,0:T(8,128)(2,1)S(1)}, u32[]{:S(2)}, u32[]{:S(2)}) collective-permute-start(bf16[288,1024]{1,0:T(8,128)(2,1)S(1)} %concatenate.65), channel_id=1, source_target_pairs={{0,16},{16,0},{1,17},{17,1},{2,18},{18,2},{3,19},{19,3},{4,20},{20... | collective-permute-start | bytes 1769480 | tf_op jit(solution)/shard_map/ppermute | solution.py:161
  103.0 20.6 %collective-permute-start.16 = (bf16[288,1152]{1,0:T(8,128)(2,1)S(1)}, bf16[288,1152]{1,0:T(8,128)(2,1)S(1)}, u32[]{:S(2)}, u32[]{:S(2)}) collective-permute-start(bf16[288,1152]{1,0:T(8,128)(2,1)S(1)} %concatenate.66), channel_id=1, source_target_pairs={{0,8},{8,0},{1,9},{9,1},{2,10},{10,2},{3,11},{11,3},{4,12},{12,4},... | collective-permute-start | bytes 1990664 | tf_op jit(solution)/shard_map/ppermute | solution.py:161
  104.2 38.0 %collective-permute-start.26 = (bf16[288,2048]{1,0:T(8,128)(2,1)S(1)}, bf16[288,2048]{1,0:T(8,128)(2,1)S(1)}, u32[]{:S(2)}, u32[]{:S(2)}) collective-permute-start(bf16[288,2048]{1,0:T(8,128)(2,1)S(1)} %pad_maximum_fusion.1), channel_id=1, source_target_pairs={{2,6},{6,4},{4,0},{0,2},{3,7},{7,5},{5,1},{1,3},{10,14},{14,12},{1... | collective-permute-start | bytes 3538952 | tf_op jit(solution)/shard_map/ppermute | solution.py:167
  123.6 16.1 %collective-permute-start.22 = (bf16[288,1024]{1,0:T(8,128)(2,1)S(1)}, bf16[288,1024]{1,0:T(8,128)(2,1)S(1)}, u32[]{:S(2)}, u32[]{:S(2)}) collective-permute-start(bf16[288,1024]{1,0:T(8,128)(2,1)S(1)} %bitcast.33), channel_id=1, source_target_pairs={{0,16},{16,0},{1,17},{17,1},{2,18},{18,2},{3,19},{19,3},{4,20},{20... | collective-permute-start | bytes 1769480 | tf_op jit(solution)/shard_map/ppermute | solution.py:161
  124.9 14.9 %collective-permute-start.23 = (bf16[288,1024]{1,0:T(8,128)(2,1)S(1)}, bf16[288,1024]{1,0:T(8,128)(2,1)S(1)}, u32[]{:S(2)}, u32[]{:S(2)}) collective-permute-start(bf16[288,1024]{1,0:T(8,128)(2,1)S(1)} %bitcast.32), channel_id=1, source_target_pairs={{0,8},{8,0},{1,9},{9,1},{2,10},{10,2},{3,11},{11,3},{4,12},{12,4},... | collective-permute-start | bytes 1769480 | tf_op jit(solution)/shard_map/ppermute | solution.py:161
  139.8 10.8 %collective-permute-start.24 = (bf16[288,1024]{1,0:T(8,128)(2,1)S(1)}, bf16[288,1024]{1,0:T(8,128)(2,1)S(1)}, u32[]{:S(2)}, u32[]{:S(2)}) collective-permute-start(bf16[288,1024]{1,0:T(8,128)(2,1)S(1)} %bitcast.27), channel_id=1, source_target_pairs={{0,16},{16,0},{1,17},{17,1},{2,18},{18,2},{3,19},{19,3},{4,20},{20... | collective-permute-start | bytes 1769480 | tf_op jit(solution)/shard_map/ppermute | solution.py:161
  140.7 22.9 %collective-permute-start.30 = (bf16[288,1024]{1,0:T(8,128)(2,1)S(1)}, bf16[288,1024]{1,0:T(8,128)(2,1)S(1)}, u32[]{:S(2)}, u32[]{:S(2)}) collective-permute-start(bf16[288,1024]{1,0:T(8,128)(2,1)S(1)} %bitcast.26), channel_id=1, source_target_pairs={{0,8},{8,0},{1,9},{9,1},{2,10},{10,2},{3,11},{11,3},{4,12},{12,4},... | collective-permute-start | bytes 1769480 | tf_op jit(solution)/shard_map/ppermute | solution.py:161
  142.8 10.9 %collective-permute-start.28 = (bf16[144,1024]{1,0:T(8,128)(2,1)S(1)}, bf16[144,1024]{1,0:T(8,128)(2,1)S(1)}, u32[]{:S(2)}, u32[]{:S(2)}) collective-permute-start(bf16[144,1024]{1,0:T(8,128)(2,1)S(1)} %slice.234), channel_id=1, source_target_pairs={{0,16},{16,0},{1,17},{17,1},{2,18},{18,2},{3,19},{19,3},{4,20},{20... | collective-permute-start | bytes 884744 | tf_op jit(solution)/shard_map/ppermute | solution.py:161
  144.1 14.9 %collective-permute-start.27 = (bf16[144,1024]{1,0:T(8,128)(2,1)S(1)}, bf16[144,1024]{1,0:T(8,128)(2,1)S(1)}, u32[]{:S(2)}, u32[]{:S(2)}) collective-permute-start(bf16[144,1024]{1,0:T(8,128)(2,1)S(1)} %slice.235), channel_id=1, source_target_pairs={{0,8},{8,0},{1,9},{9,1},{2,10},{10,2},{3,11},{11,3},{4,12},{12,4},... | collective-permute-start | bytes 884744 | tf_op jit(solution)/shard_map/ppermute | solution.py:161
  150.8 15.6 %collective-permute-start.25 = (bf16[144,1024]{1,0:T(8,128)(2,1)S(1)}, bf16[144,1024]{1,0:T(8,128)(2,1)S(1)}, u32[]{:S(2)}, u32[]{:S(2)}) collective-permute-start(bf16[144,1024]{1,0:T(8,128)(2,1)S(1)} %slice.236), channel_id=1, source_target_pairs={{0,8},{8,0},{1,9},{9,1},{2,10},{10,2},{3,11},{11,3},{4,12},{12,4},... | collective-permute-start | bytes 884744 | tf_op jit(solution)/shard_map/ppermute | solution.py:161
  159.1 15.4 %collective-permute-start.29 = (bf16[144,2048]{1,0:T(8,128)(2,1)S(1)}, bf16[144,2048]{1,0:T(8,128)(2,1)S(1)}, u32[]{:S(2)}, u32[]{:S(2)}) collective-permute-start(bf16[144,2048]{1,0:T(8,128)(2,1)S(1)} %pad_maximum_fusion.6), channel_id=1, source_target_pairs={{2,6},{6,4},{4,0},{0,2},{3,7},{7,5},{5,1},{1,3},{10,14},{14,12},{1... | collective-permute-start | bytes 1769480 | tf_op jit(solution)/shard_map/ppermute | solution.py:167
  163.8 6.8 %collective-permute-start.31 = (bf16[144,1024]{1,0:T(8,128)(2,1)S(1)}, bf16[144,1024]{1,0:T(8,128)(2,1)S(1)}, u32[]{:S(2)}, u32[]{:S(2)}) collective-permute-start(bf16[144,1024]{1,0:T(8,128)(2,1)S(1)} %slice.233), channel_id=1, source_target_pairs={{0,16},{16,0},{1,17},{17,1},{2,18},{18,2},{3,19},{19,3},{4,20},{20... | collective-permute-start | bytes 884744 | tf_op jit(solution)/shard_map/ppermute | solution.py:161
  165.6 12.6 %collective-permute-start.12 = (bf16[144,1024]{1,0:T(8,128)(2,1)S(1)}, bf16[144,1024]{1,0:T(8,128)(2,1)S(1)}, u32[]{:S(2)}, u32[]{:S(2)}) collective-permute-start(bf16[144,1024]{1,0:T(8,128)(2,1)S(1)} %slice.237), channel_id=1, source_target_pairs={{0,8},{8,0},{1,9},{9,1},{2,10},{10,2},{3,11},{11,3},{4,12},{12,4},... | collective-permute-start | bytes 884744 | tf_op jit(solution)/shard_map/ppermute | solution.py:161
  174.9 10.8 %collective-permute-start.32 = (bf16[144,2048]{1,0:T(8,128)(2,1)S(1)}, bf16[144,2048]{1,0:T(8,128)(2,1)S(1)}, u32[]{:S(2)}, u32[]{:S(2)}) collective-permute-start(bf16[144,2048]{1,0:T(8,128)(2,1)S(1)} %pad_maximum_fusion.7), channel_id=1, source_target_pairs={{2,6},{6,4},{4,0},{0,2},{3,7},{7,5},{5,1},{1,3},{10,14},{14,12},{1... | collective-permute-start | bytes 1769480 | tf_op jit(solution)/shard_map/ppermute | solution.py:167
  176.8 6.8 %collective-permute-start.33 = (bf16[144,1024]{1,0:T(8,128)(2,1)S(1)}, bf16[144,1024]{1,0:T(8,128)(2,1)S(1)}, u32[]{:S(2)}, u32[]{:S(2)}) collective-permute-start(bf16[144,1024]{1,0:T(8,128)(2,1)S(1)} %slice.232), channel_id=1, source_target_pairs={{0,16},{16,0},{1,17},{17,1},{2,18},{18,2},{3,19},{19,3},{4,20},{20... | collective-permute-start | bytes 884744 | tf_op jit(solution)/shard_map/ppermute | solution.py:161
